TPU v7x, 32 devices: a whole 2x2x4 slice. The times are simulated.
32 devices in a mesh: dp: 16 (over z, x, core), tensor: 2 (over y).
Axes of the slice: x: 2, y: 2, z: 4, core: 2. Of those that a mesh axis runs over, the one named last changes fastest.
Arguments:
- layer_in: bfloat16 [16, 2, 1024, 768], P(None, 'tensor', 'dp'), may hold values from -6 to 6
- out_grad: bfloat16 [16, 2, 1024, 768], P(None, 'tensor', 'dp'), may hold values from -6 to 6
- seq_lengths: int32 [16], replicated, may hold values from 1 to 2048, 20480 in all
- slot_perm: int32 [16], replicated, may hold values from 0 to 15, each once
- norm_gain: float32 [768], replicated, may hold values from 0.1 to 1.9
- w_gate: bfloat16 [768, 1536], P('dp', 'tensor'), may hold values from -0.21875 to 0.21875
- w_inner: bfloat16 [768, 1536], P('dp', 'tensor'), may hold values from -0.21875 to 0.21875
- w_bc: bfloat16 [768, 128], P('dp'), may hold values from -0.21875 to 0.21875
- w_dt: bfloat16 [768, 48], P('dp', 'tensor'), may hold values from -0.21875 to 0.21875
- conv_x: float32 [4, 1536], P(None, 'tensor'), may hold values from -3 to 3
- conv_bc: float32 [4, 128], replicated, may hold values from -2 to 2
- dt_bias: float32 [48], P('tensor'), may hold values from -4 to -2
- a_log: float32 [24], P('tensor'), may hold values from -4.5 to 0.5
- dskip: float32 [24], P('tensor'), may hold values from 1 to 3
- inner_gain: float32 [1536], P('tensor'), may hold values from 0.1 to 1.9
- w_out: bfloat16 [1536, 768], P('tensor', 'dp'), may hold values from -0.15625 to 0.15625
Outputs:
- output: bfloat16 [16, 2, 1024, 768], P(None, 'tensor', 'dp')
- input_grad: bfloat16 [16, 2, 1024, 768], P(None, 'tensor', 'dp')
- grad_norm_gain: float32 [768], replicated
- grad_w_gate: float32 [768, 1536], P('dp', 'tensor')
- grad_w_inner: float32 [768, 1536], P('dp', 'tensor')
- grad_w_bc: float32 [768, 128], P('dp')
- grad_w_dt: float32 [768, 48], P('dp', 'tensor')
- grad_conv_x: float32 [4, 1536], P(None, 'tensor')
- grad_conv_bc: float32 [4, 128], replicated
- grad_dt_bias: float32 [48], P('tensor')
- grad_a_log: float32 [24], P('tensor')
- grad_dskip: float32 [24], P('tensor')
- grad_inner_gain: float32 [1536], P('tensor')
- grad_w_out: float32 [1536, 768], P('tensor', 'dp')
Inputs may be any that keep to these rules, and one draw needn't show every extreme that they name: Sequence s is computed in slot slot_perm[s]; slot i belongs to index i of dp; out_grad, output and input_grad are indexed by slot. `seq_lengths`: some sequence has exactly 2048 valid positions.
All inputs are finite; a program needn't handle non-finite values.
Results may differ from a plain program's by a relative error of at most 0.011.
Values may be sent and summed in bfloat16 or wider, within the bound.
No kernel may reach another device: no remote copies, remote signals or barrier semaphores. Data moves between devices by JAX's collectives and lax.ppermute only.
A program may use at most 320 MiB of HBM per device.

v0:
```python
import jax
import jax.numpy as jnp
from jax import lax
from jax.sharding import PartitionSpec as P

BLOCK = 128
exact_prec = lax.Precision.HIGHEST


def causal_conv(values, kernel):
    taps_count = kernel.shape[0]
    length = values.shape[0]
    padded = jnp.pad(values, ((taps_count - 1, 0), (0, 0)))
    summed = jnp.zeros(values.shape, jnp.float32)
    for offset in range(taps_count):
        summed = summed + kernel[offset] * padded[offset : offset + length]
    return summed


def strict_scan(values, state_in, state_out, log_decay):
    length, head_count, head_width = values.shape
    blocks = length // BLOCK
    blocked = values.reshape(blocks, BLOCK, head_count, head_width)
    in_maps = state_in.reshape(blocks, BLOCK, -1)
    out_maps = state_out.reshape(blocks, BLOCK, -1)
    partial_sums = jnp.cumsum(log_decay.reshape(blocks, BLOCK, head_count), axis=1)
    scores = jnp.einsum("kin,kjn->kij", out_maps, in_maps, precision=exact_prec)
    row_ids = lax.broadcasted_iota(jnp.int32, (BLOCK, BLOCK), 0)
    col_ids = lax.broadcasted_iota(jnp.int32, (BLOCK, BLOCK), 1)
    lower = (row_ids > col_ids)[None, :, :, None]
    spread = partial_sums[:, :, None, :] - partial_sums[:, None, :, :]
    decay = jnp.where(lower, jnp.exp(jnp.where(lower, spread, 0.0)), 0.0)
    weights_in = scores[..., None] * decay
    inside = jnp.einsum("kijh,kjhp->kihp", weights_in, blocked, precision=exact_prec)
    to_end = jnp.exp(partial_sums[:, -1:, :] - partial_sums)
    block_states = jnp.einsum(
        "kjn,kjhp->khnp", in_maps, blocked * to_end[..., None], precision=exact_prec
    )
    block_decay = jnp.exp(partial_sums[:, -1, :])

    def carry_step(carried, item):
        decay_now, state_now = item
        return (carried * decay_now[:, None, None] + state_now, carried)

    start_state = jnp.zeros(block_states.shape[1:], jnp.float32)
    _, entering = lax.scan(carry_step, start_state, (block_decay, block_states))
    outside = jnp.einsum("kin,khnp->kihp", out_maps, entering, precision=exact_prec)
    outside = outside * jnp.exp(partial_sums)[..., None]
    return (inside + outside).reshape(length, head_count, head_width)


def mixer(
    inner_in, bc_raw, step_raw, gate, conv_x, conv_bc, dt_bias, a_log, dskip, inner_gain, mask
):
    length = inner_in.shape[0]
    head_count = a_log.shape[0]
    head_width = inner_in.shape[1] // head_count
    conv_out = jax.nn.silu(causal_conv(inner_in, conv_x))
    bc_conv = jax.nn.silu(causal_conv(bc_raw, conv_bc))
    state_width = bc_conv.shape[1] // 2
    state_in = bc_conv[:, :state_width]
    state_out = bc_conv[:, state_width:]
    step_size = jax.nn.softplus(step_raw + dt_bias).reshape(length, head_count, 2)
    log_decay = -step_size * jnp.exp(a_log)[None, :, None]
    heads_x = conv_out.reshape(length, head_count, head_width)
    forward_v = (mask[:, None] * step_size[:, :, 0])[:, :, None] * heads_x
    backward_v = (mask[:, None] * step_size[:, :, 1])[:, :, None] * heads_x
    forward_out = strict_scan(forward_v, state_in, state_out, log_decay[:, :, 0])
    backward_out = jnp.flip(
        strict_scan(
            jnp.flip(backward_v, 0),
            jnp.flip(state_in, 0),
            jnp.flip(state_out, 0),
            jnp.flip(log_decay[:, :, 1], 0),
        ),
        0,
    )
    mixture = forward_out + backward_out + dskip[None, :, None] * heads_x
    gated_out = mixture * jax.nn.silu(gate.reshape(length, head_count, head_width))
    scaled = gated_out * lax.rsqrt(jnp.mean(gated_out * gated_out, axis=-1, keepdims=True) + 1e-05)
    return (scaled * inner_gain.reshape(head_count, head_width)).reshape(
        length, head_count * head_width
    )


def project(left_operand, right_operand):
    return jnp.einsum(
        "web,bz->wez", left_operand, right_operand, preferred_element_type=jnp.float32
    )


def back_project(left_operand, right_operand):
    return jnp.einsum(
        "hkq,nq->hkn", left_operand, right_operand, preferred_element_type=jnp.float32
    )


def weight_grad(left_operand, right_operand):
    return jnp.einsum(
        "rno,rnm->om", left_operand, right_operand, preferred_element_type=jnp.float32
    )


def shards(
    layer_in,
    out_grad,
    seq_lengths,
    slot_perm,
    norm_gain,
    w_gate,
    w_inner,
    w_bc,
    w_dt,
    conv_x,
    conv_bc,
    dt_bias,
    a_log,
    dskip,
    inner_gain,
    w_out,
):
    dp_count = lax.axis_size("dp")
    rank_dp = lax.axis_index("dp")
    rank_tensor = lax.axis_index("tensor")
    seq_total = slot_perm.shape[0]
    seq_dev = seq_total // dp_count
    sender = jnp.argsort(slot_perm)
    placed_in = jnp.take(layer_in, sender, axis=0)
    local_in, local_grad = (
        lax.all_to_all(placed_in, "dp", split_axis=0, concat_axis=2, tiled=True),
        lax.all_to_all(out_grad, "dp", split_axis=0, concat_axis=2, tiled=True),
    )
    rows_half = local_in[:, 0].astype(jnp.float32)
    cot_half = local_grad[:, 0].astype(jnp.float32)
    half_len = rows_half.shape[1]
    full_len = half_len * lax.axis_size("tensor")
    mine = lax.dynamic_slice_in_dim(sender, rank_dp * seq_dev, seq_dev)
    my_lengths = jnp.take(seq_lengths, mine)
    positions = jnp.arange(full_len, dtype=jnp.int32)
    mask_full = (positions[None, :] < my_lengths[:, None]).astype(jnp.float32)
    mask_half = lax.dynamic_slice_in_dim(mask_full, rank_tensor * half_len, half_len, 1)
    inv_rms = lax.rsqrt(jnp.mean(rows_half * rows_half, axis=-1, keepdims=True) + 1e-05)
    unit_rows = rows_half * inv_rms
    normed_half = (unit_rows * norm_gain).astype(jnp.bfloat16)
    normed = lax.all_gather(normed_half, "tensor", axis=1, tiled=True)
    gate_w, inner_w, bc_w, dt_w, output_weight = (
        lax.all_gather(w_gate, "dp", axis=0, tiled=True),
        lax.all_gather(w_inner, "dp", axis=0, tiled=True),
        lax.all_gather(w_bc, "dp", axis=0, tiled=True),
        lax.all_gather(w_dt, "dp", axis=0, tiled=True),
        lax.all_gather(w_out, "dp", axis=1, tiled=True),
    )
    gate = project(normed, gate_w)
    inner_in = project(normed, inner_w)
    bc_raw = project(normed, bc_w)
    step_raw = project(normed, dt_w)

    def local_mixer(
        inner_val,
        bc_val,
        step_val,
        gate_val,
        convx_val,
        convbc_val,
        bias_val,
        alog_val,
        skip_val,
        gain_val,
    ):
        return jax.vmap(mixer, in_axes=(0, 0, 0, 0, None, None, None, None, None, None, 0))(
            inner_val,
            bc_val,
            step_val,
            gate_val,
            convx_val,
            convbc_val,
            bias_val,
            alog_val,
            skip_val,
            gain_val,
            mask_full,
        )

    mixed_out, pull_mixer = jax.vjp(
        local_mixer,
        inner_in,
        bc_raw,
        step_raw,
        gate,
        conv_x,
        conv_bc,
        dt_bias,
        a_log,
        dskip,
        inner_gain,
    )
    mixed_reduced = mixed_out.astype(jnp.bfloat16)
    cot_masked = (cot_half * mask_half[..., None]).astype(jnp.bfloat16)
    cotangent_whole = lax.all_gather(cot_masked, "tensor", axis=1, tiled=True)
    partial_row_block = jnp.einsum(
        "mtu,ur->mtr", mixed_reduced, output_weight, preferred_element_type=jnp.float32
    )
    mixed_half = lax.psum_scatter(partial_row_block, "tensor", scatter_dimension=1, tiled=True)
    gradient_whole = jnp.einsum(
        "mbn,pn->mbp", cotangent_whole, output_weight, preferred_element_type=jnp.float32
    )
    grad_mixed = lax.optimization_barrier(gradient_whole.astype(jnp.bfloat16)).astype(jnp.float32)
    output_local = jnp.einsum(
        "thw,thz->wz", mixed_reduced, cotangent_whole, preferred_element_type=jnp.float32
    )
    (
        grad_inner,
        grad_bc_part,
        grad_step,
        grad_gate,
        grad_convx,
        grad_convbc,
        grad_bias,
        grad_alog,
        grad_skip,
        grad_gain,
    ) = pull_mixer(grad_mixed)
    gate_low = grad_gate.astype(jnp.bfloat16)
    inner_low = grad_inner.astype(jnp.bfloat16)
    step_low = grad_step.astype(jnp.bfloat16)
    normed_part = back_project(gate_low, gate_w) + back_project(inner_low, inner_w)
    normed_part = normed_part + back_project(step_low, dt_w)
    normed_grad, bc_grad = (
        lax.psum_scatter(normed_part, "tensor", scatter_dimension=1, tiled=True),
        lax.psum_scatter(grad_bc_part, "tensor", scatter_dimension=1, tiled=True),
    )
    bc_low = bc_grad.astype(jnp.bfloat16)
    normed_grad = normed_grad + back_project(bc_low, bc_w)
    gate_wgrad = weight_grad(normed, gate_low)
    inner_wgrad = weight_grad(normed, inner_low)
    step_wgrad = weight_grad(normed, step_low)
    bc_wgrad = weight_grad(normed_half, bc_low)
    scaled_grad = normed_grad * norm_gain
    norm_part = jnp.sum(normed_grad * unit_rows, axis=(0, 1))
    rows_grad = cot_half + inv_rms * (
        scaled_grad - unit_rows * jnp.mean(scaled_grad * unit_rows, axis=-1, keepdims=True)
    )
    gate_sum, inner_sum, step_sum, out_sum = (
        lax.psum_scatter(gate_wgrad, "dp", scatter_dimension=0, tiled=True),
        lax.psum_scatter(inner_wgrad, "dp", scatter_dimension=0, tiled=True),
        lax.psum_scatter(step_wgrad, "dp", scatter_dimension=0, tiled=True),
        lax.psum_scatter(output_local, "dp", scatter_dimension=1, tiled=True),
    )
    bc_all, norm_all, convbc_all = lax.psum((bc_wgrad, norm_part, grad_convbc), ("dp", "tensor"))
    bc_rows = w_bc.shape[0]
    bc_sum = lax.dynamic_slice_in_dim(bc_all, rank_dp * bc_rows, bc_rows, 0)
    convx_sum, bias_sum, alog_sum, skip_sum, gain_sum = lax.psum(
        (grad_convx, grad_bias, grad_alog, grad_skip, grad_gain), "dp"
    )
    out_half = rows_half + mask_half[..., None] * mixed_half
    output, input_grad = (
        lax.all_to_all(
            out_half.astype(jnp.bfloat16)[:, None], "dp", split_axis=2, concat_axis=0, tiled=True
        ),
        lax.all_to_all(
            rows_grad.astype(jnp.bfloat16)[:, None], "dp", split_axis=2, concat_axis=0, tiled=True
        ),
    )
    return (
        output,
        input_grad,
        norm_all,
        gate_sum,
        inner_sum,
        bc_sum,
        step_sum,
        convx_sum,
        convbc_all,
        bias_sum,
        alog_sum,
        skip_sum,
        gain_sum,
        out_sum,
    )


def solution(mesh):
    return jax.shard_map(
        shards,
        mesh=mesh,
        in_specs=(
            P(None, "tensor", "dp", None),
            P(None, "tensor", "dp", None),
            P(),
            P(),
            P(),
            P("dp", "tensor"),
            P("dp", "tensor"),
            P("dp", None),
            P("dp", "tensor"),
            P(None, "tensor"),
            P(),
            P("tensor"),
            P("tensor"),
            P("tensor"),
            P("tensor"),
            P("tensor", "dp"),
        ),
        out_specs=(
            P(None, "tensor", "dp", None),
            P(None, "tensor", "dp", None),
            P(),
            P("dp", "tensor"),
            P("dp", "tensor"),
            P("dp", None),
            P("dp", "tensor"),
            P(None, "tensor"),
            P(),
            P("tensor"),
            P("tensor"),
            P("tensor"),
            P("tensor"),
            P("tensor", "dp"),
        ),
        check_vma=False,
    )
```

profile of v0, /device:TPU:0, one launch (start us, length us, event | category | flops | bytes accessed | tf_op | source)
XLA Modules:
  0.0 1662.7 jit_solution(1774268298412946500)
XLA Ops:
  10.7 43.2 %all_to_all.42 = bf16[16,1,64,768]{3,2,1,0:T(8,128)(2,1)S(1)} all-to-all(bf16[16,1,64,768]{3,2,1,0:T(8,128)(2,1)S(1)} %bitcast_select_fusion), channel_id=1, replica_groups=mesh['dp'=16,'tensor'=2] {'dp'}, dimensions={0} | all-to-all | bytes 3145728 | tf_op jit(solution)/shard_map/all_to_all | solution.py:130
  67.4 38.5 %all-gather = bf16[16,48,24]{1,2,0:T(8,128)(2,1)S(1)} all-gather(bf16[1,48,24]{1,2,0:T(8,128)(2,1)} %bitcast.685), channel_id=1, replica_groups=mesh['dp'=16,'tensor'=2] {'dp'}, dimensions={0}, use_global_device_ids=true | all-gather | bytes 39168 | tf_op jit(solution)/shard_map/all_gather | solution.py:150
  109.4 26.3 %all_gather.24 = bf16[768,128]{1,0:T(8,128)(2,1)} all-gather(bf16[48,128]{1,0:T(8,128)(2,1)S(1)} %copy-done.93), channel_id=1, replica_groups=mesh['dp'=16,'tensor'=2] {'dp'}, dimensions={0}, use_global_device_ids=true | all-gather | bytes 208896 | tf_op jit(solution)/shard_map/all_gather | solution.py:149
  216.5 34.1 %while.69 = (s32[]{:T(128)}, f32[1,12,64,64]{3,2,1,0:T(8,128)S(1)}, f32[16,1,12,64,64]{4,3,2,1,0:T(8,128)}, f32[16,1,12,1,1]{2,4,3,1,0:T(1,128)S(1)}, f32[16,1,1...) while((s32[]{:T(128)}, f32[1,12,64,64]{3,2,1,0:T(8,128)S(1)}, ...), condition=%wide.region_4.5_spmd.clone, body=%wide.region_3.4_spmd.clone.sunk | while | flops 196611 | bytes 1967868 | solution.py:46
  319.0 54.7 %while.70 = (s32[]{:T(128)}, f32[1,12,64,64]{3,2,1,0:T(8,128)S(1)}, f32[16,1,12,64,64]{4,3,2,1,0:T(8,128)}, f32[16,1,12,1,1]{2,4,3,1,0:T(1,128)S(1)}, f32[16,1,1...) while((s32[]{:T(128)}, f32[1,12,64,64]{3,2,1,0:T(8,128)S(1)}, ...), condition=%wide.region_7.8_spmd.clone, body=%wide.region_6.7_spmd.clone.sunk | while | flops 196611 | bytes 1967404 | solution.py:46
  394.6 30.4 %bitcast_add_fusion.6 = f32[1,16,128,12,64]{2,4,3,1,0:T(8,128)} fusion(f32[16,128,12,64]{1,3,2,0:T(8,128)} %bitcast.637, f32[16,128,12]{1,2,0:T(8,128)S(1)} %copy.646, f32[16,128,12]{1,2,0:T(8,128)S(1)} %copy.636, f32[16,128,128]{2,1,0:T(8,128)} %fusion.217, pred[128,128]{1,0:T(8,128)(4,1)S(1)} %copy-done.91, f32[16,128,12,64]{1,0,3,2:T(8,128)} %bitcast.604), kind=kOutput, calls=%fused_computation.67 | convolution fusion | flops 2431647744 | bytes 20135936 | tf_op jit(solution)/shard_map/jvp(vmap(kijh,kjhp->kihp))/dot_general | solution.py:34
  424.9 29.2 %bitcast_add_fusion.7 = f32[1,16,128,12,64]{2,4,3,1,0:T(8,128)} fusion(f32[16,128,12,64]{1,3,2,0:T(8,128)S(1)} %bitcast.635, f32[16,128,12]{1,2,0:T(8,128)S(1)} %copy.628, f32[16,128,12]{1,2,0:T(8,128)S(1)} %copy.618, f32[16,128,128]{2,1,0:T(8,128)S(1)} %copy-done.46, pred[128,128]{1,0:T(8,128)(4,1)S(1)} %copy-done.91, ...), kind=kOutput, calls=%fused_computation.68 | convolution fusion | flops 2431647744 | bytes 20135936 | tf_op jit(solution)/shard_map/jvp(vmap(kijh,kjhp->kihp))/dot_general | solution.py:34
  454.8 16.1 copy.672
  512.4 13.8 multiply_reduce_fusion.11
  593.1 51.8 %while.71 = (s32[]{:T(128)}, f32[1,12,64,64]{3,2,1,0:T(8,128)S(1)}, f32[16,1,12]{2,1,0:T(1,128)S(1)}, f32[16,1,12,64,64]{4,3,2,1,0:T(8,128)}, f32[16,1,12,64,64]...) while((s32[]{:T(128)}, f32[1,12,64,64]{3,2,1,0:T(8,128)S(1)}, ...), condition=%wide.region_13.14_spmd.clone, body=%wide.region_11.13_spmd.clone.sunk | while | flops 294904 | bytes 2164048 | solution.py:46
  645.0 15.9 fusion.37
  684.6 61.6 %while.72 = (s32[]{:T(128)}, f32[1,12,64,64]{3,2,1,0:T(8,128)S(1)}, f32[16,1,12]{2,1,0:T(1,128)S(1)}, f32[16,1,12,64,64]{4,3,2,1,0:T(8,128)}, f32[16,1,12,64,64]...) while((s32[]{:T(128)}, f32[1,12,64,64]{3,2,1,0:T(8,128)S(1)}, ...), condition=%wide.region_16.17_spmd.clone, body=%wide.region_14.16_spmd.clone.sunk | while | flops 294904 | bytes 2164048 | solution.py:46
  758.7 27.0 %fusion.62 = f32[16,12,128,128]{3,2,1,0:T(8,128)} fusion(f32[16,12,64,128]{3,0,2,1:T(8,128)S(1)} %bitcast.583, f32[16,128,12,64]{1,0,3,2:T(8,128)} %get-tuple-element.851), kind=kOutput, calls=%fused_computation.126 | convolution fusion | flops 2415919104 | bytes 25165824 | tf_op jit(solution)/shard_map/transpose(jvp(vmap(kijh,kjhp->kihp)))/dot_general | solution.py:34
  785.7 19.3 %fusion.36 = (f32[16,128,12]{1,2,0:T(8,128)S(1)}, f32[16,128,12]{1,2,0:T(8,128)}, f32[1,16,128,12,64]{2,4,3,1,0:T(8,128)}) fusion(f32[16,12,64,128]{3,2,1,0:T(8,128)S(1)} %fusion.30, f32[1,16,128,12,64]{2,1,0,4,3:T(8,128)S(1)} %bitcast.656, f32[16,128,12]{1,2,0:T(8,128)S(1)} %copy-done.63, f32[16,128,12]{1,2,0:T(8,128)S(1)} %copy-done.58, ...), kind=kOutput, calls=%fused_computation.79 | convolution fusion | flops 2439462912 | bytes 26722304 | tf_op jit(solution)/shard_map/transpose(jvp(vmap(kijh,kjhp->kihp)))/dot_general | solution.py:34
  863.5 17.6 %bitcast_add_fusion.5 = f32[1,16,128,12,64]{2,4,3,1,0:T(8,128)S(1)} fusion(f32[16,12,64,128]{3,2,1,0:T(8,128)} %get-tuple-element.904, f32[16,128,12]{1,2,0:T(8,128)S(1)} %copy-done.62, f32[16,128,12]{1,2,0:T(8,128)S(1)} %copy-done.61, f32[16,128,128]{2,1,0:T(8,128)S(1)} %copy-done.48, pred[128,128]{1,0:T(8,128)(4,1)S(1)} %copy-done.92, ...), kind=kOutput, calls=%fused_computation.66 | convolution fusion | flops 2431647744 | bytes 20135936 | tf_op jit(solution)/shard_map/transpose(jvp(vmap(kijh,kjhp->kihp)))/dot_general | solution.py:34
  924.8 42.1 %fusion.19 = (f32[16,128,12]{1,2,0:T(8,128)}, f32[16,128,12]{1,2,0:T(8,128)}, f32[16,128,128]{2,1,0:T(8,128)}, f32[16,128,128]{2,1,0:T(8,128)}, f32[16,128,12]{1,2,0:T(8,128)}, /*index=5*/f32[16,128,12]{1,2,0:T(8,128)}) fusion(f32[16,128,12]{1,2,0:T(8,128)S(1)} %copy-done.61, f32[16,128,128]{2,1,0:T(8,128)} %fusion.217, ...), kind=kOutput, calls=%fused_computation.53 | convolution fusion | flops 2484502528 | bytes 29966336 | tf_op jit(solution)/shard_map/transpose(jvp(vmap(kijh,kjhp->kihp)))/dot_general | solution.py:34
  1049.7 14.8 multiply_reduce_fusion.4
  1117.1 43.6 %reduce-scatter.12.cloned.1.call-done = f32[1,1024,768]{2,1,0:T(8,128)} async-done(((f32[1,2048,768]{2,1,0:T(8,128)}), f32[1,1024,768]{2,1,0:T(8,128)}) %reduce-scatter.12.cloned.1.call-update) | async-done | bytes 3145744 | tf_op jit(solution)/shard_map/reduce_scatter | solution.py:229
  1166.2 73.9 %reduce-scatter.10.cloned.1.call-done = f32[1,1024,768]{2,1,0:T(8,128)} async-done(((f32[1,2048,768]{2,1,0:T(8,128)}), f32[1,1024,768]{2,1,0:T(8,128)}) %reduce-scatter.10.cloned.1.call-update) | async-done | bytes 3145744 | tf_op jit(solution)/shard_map/reduce_scatter | solution.py:203
  1311.7 82.6 %all-reduce.29 = (f32[4,768]{1,0:T(4,128)}, f32[24]{0:T(128)}, f32[12]{0:T(128)}, f32[12]{0:T(128)}, f32[768]{0:T(1024)}) all-reduce(f32[4,768]{1,0:T(4,128)S(1)} %pad_add_fusion.7, f32[24]{0:T(128)S(1)} %get-tuple-element.843, f32[12]{0:T(128)S(1)} %exponential_multiply_fusion, ...), channel_id=1, replica_groups=mesh['dp'=16,'tensor'=2] {'dp'}, use_global_device_ids=true, to_apply=%region_46.47 | all-reduce | flops 3888 | bytes 31104 | tf_op jit(solution)/shard_map/psum | solution.py:252
  1395.8 59.7 %all-reduce.32.cloned.1.call-done = f32[768,128]{1,0:T(8,128)} async-done(((f32[768,128]{1,0:T(8,128)}), f32[768,128]{1,0:T(8,128)}) %all-reduce.32.cloned.1.call-update) | async-done | bytes 393232 | tf_op jit(solution)/shard_map/psum | solution.py:249
  1456.9 39.4 %all-reduce.28 = (f32[768]{0:T(1024)}, f32[4,128]{1,0:T(4,128)}) all-reduce(f32[768]{0:T(1024)S(1)} %get-tuple-element.766, f32[4,128]{1,0:T(4,128)S(1)} %pad_add_fusion.8), channel_id=1, replica_groups=mesh['dp'=16,'tensor'=2] {'dp','tensor'}, use_global_device_ids=true, to_apply=%region_37.38 | all-reduce | flops 1280 | bytes 10240 | tf_op jit(solution)/shard_map/psum | solution.py:249
  1523.0 66.2 %reduce-scatter.16.cloned.1.call-done = f32[48,768]{1,0:T(8,128)} async-done(((f32[768,768]{1,0:T(8,128)}), f32[48,768]{1,0:T(8,128)}) %reduce-scatter.16.cloned.1.call-update) | async-done | bytes 147472 | tf_op jit(solution)/shard_map/reduce_scatter | solution.py:244
  1589.2 66.8 %reduce-scatter.20.cloned.1.call-done = f32[768,48]{0,1:T(8,128)} async-done(((f32[768,768]{0,1:T(8,128)}), f32[768,48]{0,1:T(8,128)}) %reduce-scatter.20.cloned.1.call-update) | async-done | bytes 147472 | tf_op jit(solution)/shard_map/reduce_scatter | solution.py:247
  (865 shorter events, 875.8 us)
Async XLA Ops:
  7.2 134.2 %all-gather.7.cloned.1.call-start = ((), (), s32[]{:S(2)}) async-start(), calls=%async_computation.11 | async-start | bytes 4718592 | tf_op jit(solution)/shard_map/all_gather | solution.py:145
  57.0 103.9 %all-gather.9.cloned.1.call-start = ((), (), s32[]{:S(2)}) async-start(), calls=%async_computation.12 | async-start | bytes 1253376 | tf_op jit(solution)/shard_map/all_gather | solution.py:148
  57.8 449.5 %all-gather.11.cloned.1.call-start = ((), (), s32[]{:S(2)}) async-start(), calls=%async_computation.13 | async-start | bytes 1253376 | tf_op jit(solution)/shard_map/all_gather | solution.py:147
  58.5 80.7 %all-to-all-start.2 = ((bf16[16,1,64,768]{3,2,1,0:T(8,128)(2,1)}), bf16[16,1,64,768]{3,2,1,0:T(8,128)(2,1)S(1)}, u32[]{:S(2)}, u32[]{:S(2)}) async-start(bf16[16,1,64,768]{3,2,1,0:T(8,128)(2,1)} %param.25), calls=%async_computation.3 | async-start | bytes 3145728 | tf_op jit(solution)/shard_map/all_to_all | solution.py:131
  63.5 462.7 %all-gather.13.cloned.1.call-start = ((), (), s32[]{:S(2)}) async-start(), calls=%async_computation.14 | async-start | bytes 1253376 | tf_op jit(solution)/shard_map/all_gather | solution.py:151
  64.1 462.1 %all-gather.15.cloned.1.call-start = ((), (), s32[]{:S(2)}) async-start(), calls=%async_computation.16 | async-start | bytes 4718592 | tf_op jit(solution)/shard_map/all_gather | solution.py:199
  140.9 959.4 %reduce-scatter.14.cloned.1.call-start = ((), (), s32[]{:S(2)}) async-start(), calls=%async_computation.18 | async-start | bytes 1572864 | tf_op jit(solution)/shard_map/reduce_scatter | solution.py:230
  159.7 143.0 %copy-start.69 = (f32[16,12]{1,0:T(8,128)}, f32[16,12]{1,0:T(8,128)S(1)}, u32[]{:S(2)}) copy-start(f32[16,12]{1,0:T(8,128)S(1)} %get-tuple-element.878) | copy-start | bytes 2308
  160.8 115.7 %copy-start.42 = (f32[2048,12]{0,1:T(8,128)}, f32[2048,12]{0,1:T(8,128)S(1)}, u32[]{:S(2)}) copy-start(f32[2048,12]{0,1:T(8,128)S(1)} %get-tuple-element.883) | copy-start | bytes 294916
  192.0 79.6 %copy-start.9 = (f32[1,2048,64]{2,1,0:T(8,128)}, f32[1,2048,64]{2,1,0:T(8,128)S(1)}, u32[]{:S(2)}) copy-start(f32[1,2048,64]{2,1,0:T(8,128)S(1)} %get-tuple-element.880) | copy-start | bytes 1572868
  276.6 148.4 %copy-start.57 = (f32[16,128,12]{1,2,0:T(8,128)}, f32[16,128,12]{1,2,0:T(8,128)S(1)}, u32[]{:S(2)}) copy-start(f32[16,128,12]{1,2,0:T(8,128)S(1)} %copy.618) | copy-start | bytes 294916
  392.8 187.4 %copy-start.40 = (f32[16,128,12]{1,2,0:T(8,128)}, f32[16,128,12]{1,2,0:T(8,128)S(1)}, u32[]{:S(2)}) copy-start(f32[16,128,12]{1,2,0:T(8,128)S(1)} %copy.646) | copy-start | bytes 294916
  1049.6 111.1 %reduce-scatter.12.cloned.1.call-start = ((), (), s32[]{:S(2)}) async-start(), calls=%async_computation.17 | async-start | bytes 9437184 | tf_op jit(solution)/shard_map/reduce_scatter | solution.py:229
  1086.1 153.9 %reduce-scatter.10.cloned.1.call-start = ((), (), s32[]{:S(2)}) async-start(), calls=%async_computation.15 | async-start | bytes 9437184 | tf_op jit(solution)/shard_map/reduce_scatter | solution.py:203
  1094.7 299.7 %reduce-scatter.22.cloned.1.call-start = ((), (), s32[]{:S(2)}) async-start(), calls=%async_computation.23 | async-start | bytes 417792
  1100.2 355.3 %all-reduce.32.cloned.1.call-start = ((), (), s32[]{:S(2)}) async-start(), calls=%async_computation.21 | async-start | bytes 786432 | tf_op jit(solution)/shard_map/psum | solution.py:249
  1102.7 420.3 %reduce-scatter.18.cloned.1.call-start = ((), (), s32[]{:S(2)}) async-start(), calls=%async_computation.20 | async-start | bytes 2506752 | tf_op jit(solution)/shard_map/reduce_scatter | solution.py:245
  1109.7 479.4 %reduce-scatter.16.cloned.1.call-start = ((), (), s32[]{:S(2)}) async-start(), calls=%async_computation.19 | async-start | bytes 2506752 | tf_op jit(solution)/shard_map/reduce_scatter | solution.py:244
  1117.0 123.0 %copy-start.30 = (bf16[16,1,64,768]{3,2,1,0:T(8,128)(2,1)S(1)}, bf16[16,1,64,768]{3,2,1,0:T(8,128)(2,1)}, u32[]{:S(2)}) copy-start(bf16[16,1,64,768]{3,2,1,0:T(8,128)(2,1)} %copy-done.29) | copy-start | bytes 4718596
  1117.0 123.0 %copy-start.79 = (f32[1,1024]{1,0:T(1,128)S(1)}, f32[1,1024]{1,0:T(1,128)}, u32[]{:S(2)}) copy-start(f32[1,1024]{1,0:T(1,128)} %copy-done.78) | copy-start | bytes 12292
  1262.9 39.1 %all-to-all-start.3 = ((bf16[16,2,24576]{2,1,0:T(2,128)(2,1)}), bf16[16,2,24576]{2,1,0:T(2,128)(2,1)S(1)}, u32[]{:S(2)}, u32[]{:S(2)}) async-start(bf16[16,2,24576]{2,1,0:T(2,128)(2,1)} %reshape.1527), calls=%async_computation.6 | async-start | bytes 3145728 | tf_op jit(solution)/shard_map/all_to_all | solution.py:260
  1268.5 387.5 %reduce-scatter.20.cloned.1.call-start = ((), (), s32[]{:S(2)}) async-start(), calls=%async_computation.22 | async-start | bytes 2506752 | tf_op jit(solution)/shard_map/reduce_scatter | solution.py:247
  1302.0 203.9 %all-to-all-start.1 = ((bf16[16,2,24576]{2,1,0:T(2,128)(2,1)}), bf16[16,2,24576]{2,1,0:T(2,128)(2,1)}, u32[]{:S(2)}, u32[]{:S(2)}) async-start(bf16[16,2,24576]{2,1,0:T(2,128)(2,1)} %reshape.1525), calls=%async_computation.2 | async-start | bytes 3145728 | tf_op jit(solution)/shard_map/all_to_all | solution.py:257
  1502.5 153.5 %copy-start.1 = (bf16[16,1,64,768]{3,2,1,0:T(8,128)(2,1)S(1)}, bf16[16,1,64,768]{3,2,1,0:T(8,128)(2,1)}, u32[]{:S(2)}) copy-start(bf16[16,1,64,768]{3,2,1,0:T(8,128)(2,1)} %param.24) | copy-start | bytes 4718596
  (113 other events, 1832.3 us)
Sparse Core Ops, SparseCore 0:
  57.1 45.2 all-gather.6
  104.7 38.4 all-gather.8
  145.5 37.3 all-gather.10
  185.0 37.2 all-gather.12
  224.3 43.8 all-gather.14
  1049.7 17.6 reduce-scatter.13
  1086.3 74.3 reduce-scatter.11
  1163.0 77.0 reduce-scatter.9
  1243.9 71.1 reduce-scatter.21
  1320.3 135.1 all-reduce.31
  1460.3 62.5 reduce-scatter.17
  1527.2 61.9 reduce-scatter.15
  1594.0 61.9 reduce-scatter.19
where the time goes:
time: 1680 us; the launch traced here: 1660 us
  local copies, waits for them, and re-layouts  414 us (25%)
  matrix products  390 us (23%)
  waiting for transfers between devices  325 us (19%)
  other arithmetic  260 us (15%)
  blocking collectives  230 us (14%)
  starting transfers between devices  21.6 us (1%)
  between operations  18.3 us (1%)
    dot_general x6, matrix products, strict_scan(): jnp.einsum('kijh,kjhp->kihp', weights_in, blocked, precision=exact_prec)  165 us
    psum x1, blocking collectives, shards(): lax.psum((grad_convx, grad_bias, grad_alog, grad_skip, grad_gain), 'dp')  82.6 us
    dynamic_slice x128, local copies, waits for them, and re-layouts, strict_scan(): _, entering = lax.scan(carry_step, start_state, (block_decay, block_states))  75.8 us
    reduce_scatter x1, waiting for transfers between devices, shards(): lax.psum_scatter(partial_row_block, 'tensor', scatter_dimension=1, tiled=...  73.9 us
    reduce_scatter x1, waiting for transfers between devices, shards(): lax.psum_scatter(output_local, 'dp', scatter_dimension=1, tiled=True)  66.8 us
    reduce_scatter x1, waiting for transfers between devices, shards(): lax.psum_scatter(gate_wgrad, 'dp', scatter_dimension=0, tiled=True)  66.2 us
    dot_general x6, matrix products, strict_scan(): jnp.einsum('kjn,kjhp->khnp', in_maps, blocked * to_end[..., None], precis...  66 us
    psum x1, waiting for transfers between devices, shards(): lax.psum((bc_wgrad, norm_part, grad_convbc), ('dp', 'tensor'))  59.7 us
  transfers between devices with their start and end apart: 16, of which 7 were waited for; matrix products, arithmetic and copies ran while one was open for 32% of the time, Pallas kernels for 0%

commit v1 on v0

--- a/solution.py
+++ b/solution.py
@@ -246,7 +246,9 @@
         lax.psum_scatter(step_wgrad, "dp", scatter_dimension=0, tiled=True),
         lax.psum_scatter(output_local, "dp", scatter_dimension=1, tiled=True),
     )
-    bc_all, norm_all, convbc_all = lax.psum((bc_wgrad, norm_part, grad_convbc), ("dp", "tensor"))
+    bc_all, norm_all, convbc_all = lax.psum(
+        lax.psum((bc_wgrad, norm_part, grad_convbc), "tensor"), "dp"
+    )
     bc_rows = w_bc.shape[0]
     bc_sum = lax.dynamic_slice_in_dim(bc_all, rank_dp * bc_rows, bc_rows, 0)
     convx_sum, bias_sum, alog_sum, skip_sum, gain_sum = lax.psum(

time: 1680 us -> 1680 us (level)
  blocking collectives: 230 us -> 172 us
  waiting for transfers between devices: 325 us -> 366 us
  other arithmetic: 260 us -> 287 us
    psum x2, blocking collectives: 122 us -> 63.1 us  [the longest x1 58.2 us: shards(): lax.psum(lax.psum((bc_wgrad, norm_part, grad_convbc), 'tensor'), 'dp')]
    psum x1 -> x2, waiting for transfers between devices: 59.7 us -> 105 us  [the longest x1 103 us: shards(): lax.psum(lax.psum((bc_wgrad, norm_part, grad_convbc), 'tensor'), 'dp')]
    reduce_scatter x1, waiting for transfers between devices: 43.6 us -> 64.2 us  [shards(): lax.psum_scatter(normed_part, 'tensor', scatter_dimension=1, tiled=True)]
    reduce_scatter x1, waiting for transfers between devices: 66.2 us -> 45.7 us  [shards(): lax.psum_scatter(gate_wgrad, 'dp', scatter_dimension=0, tiled=True)]
    another operation x4, other arithmetic: 14.9 us -> 32.3 us  [strict_scan(): jnp.cumsum(log_decay.reshape(blocks, BLOCK, head_count), axis=1)]
    unnamed x258 -> x306, local copies, waits for them, and re-layouts: 56.8 us -> 55.4 us
  transfers between devices with their start and end apart: 16 -> 17, of which waited for: 7 -> 7; matrix products, arithmetic and copies ran while one was open for 32% -> 36% of each run, Pallas kernels for 0% -> 0%
where the time goes in v1:
time: 1680 us; the launch traced here: 1670 us
  local copies, waits for them, and re-layouts  403 us (24%)
  matrix products  401 us (24%)
  waiting for transfers between devices  366 us (22%)
  other arithmetic  287 us (17%)
  blocking collectives  172 us (10%)
  starting transfers between devices  21.3 us (1%)
  between operations  18.8 us (1%)
    dot_general x6, matrix products, strict_scan(): jnp.einsum('kijh,kjhp->kihp', weights_in, blocked, precision=exact_prec)  166 us
    psum x1, waiting for transfers between devices, shards(): lax.psum(lax.psum((bc_wgrad, norm_part, grad_convbc), 'tensor'), 'dp')  103 us
    dynamic_slice x128, local copies, waits for them, and re-layouts, strict_scan(): _, entering = lax.scan(carry_step, start_state, (block_decay, block_states))  75.8 us
    reduce_scatter x1, waiting for transfers between devices, shards(): lax.psum_scatter(partial_row_block, 'tensor', scatter_dimension=1, tiled=...  73.9 us
    dot_general x6, matrix products, strict_scan(): jnp.einsum('kjn,kjhp->khnp', in_maps, blocked * to_end[..., None], precis...  72 us
    reduce_scatter x1, waiting for transfers between devices, shards(): lax.psum_scatter(output_local, 'dp', scatter_dimension=1, tiled=True)  66.3 us
    reduce_scatter x1, waiting for transfers between devices, shards(): lax.psum_scatter(normed_part, 'tensor', scatter_dimension=1, tiled=True)  64.2 us
    psum x1, blocking collectives, shards(): lax.psum(lax.psum((bc_wgrad, norm_part, grad_convbc), 'tensor'), 'dp')  58.2 us
  transfers between devices with their start and end apart: 17, of which 7 were waited for; matrix products, arithmetic and copies ran while one was open for 36% of the time, Pallas kernels for 0%

profile of v1, /device:TPU:0, one launch (start us, length us, event | category | flops | bytes accessed | tf_op | source)
XLA Modules:
  0.0 1671.6 jit_solution(4122595757990117091)
XLA Ops:
  10.2 43.2 %all_to_all.42 = bf16[16,1,64,768]{3,2,1,0:T(8,128)(2,1)S(1)} all-to-all(bf16[16,1,64,768]{3,2,1,0:T(8,128)(2,1)S(1)} %bitcast_select_fusion), channel_id=1, replica_groups=mesh['dp'=16,'tensor'=2] {'dp'}, dimensions={0} | all-to-all | bytes 3145728 | tf_op jit(solution)/shard_map/all_to_all | solution.py:130
  66.4 39.1 %all-gather = bf16[16,48,24]{1,2,0:T(8,128)(2,1)S(1)} all-gather(bf16[1,48,24]{1,2,0:T(8,128)(2,1)S(1)} %bitcast.683), channel_id=1, replica_groups=mesh['dp'=16,'tensor'=2] {'dp'}, dimensions={0}, use_global_device_ids=true | all-gather | bytes 39168 | tf_op jit(solution)/shard_map/all_gather | solution.py:150
  107.6 26.2 %all_gather.24 = bf16[768,128]{1,0:T(8,128)(2,1)} all-gather(bf16[48,128]{1,0:T(8,128)(2,1)S(1)} %copy-done.112), channel_id=1, replica_groups=mesh['dp'=16,'tensor'=2] {'dp'}, dimensions={0}, use_global_device_ids=true | all-gather | bytes 208896 | tf_op jit(solution)/shard_map/all_gather | solution.py:149
  145.1 23.8 %fusion.213 = f32[1,16,128,12]{3,1,2,0:T(8,128)S(1)} fusion(f32[1,16,128,12]{3,1,2,0:T(8,128)S(1)} %copy.616), kind=kOutput, calls=%fused_computation.343 | output fusion | flops 3121152 | bytes 196608 | tf_op jit(solution)/shard_map/jvp(vmap(jit(cumsum)))/reduce_window_sum | solution.py:26
  233.0 54.6 %while.69 = (s32[]{:T(128)}, f32[1,12,64,64]{3,2,1,0:T(8,128)S(1)}, f32[16,1,12,64,64]{4,3,2,1,0:T(8,128)}, f32[16,1,12,1,1]{2,4,3,1,0:T(1,128)S(1)}, f32[16,1,1...) while((s32[]{:T(128)}, f32[1,12,64,64]{3,2,1,0:T(8,128)S(1)}, ...), condition=%wide.region_4.5_spmd.clone, body=%wide.region_3.4_spmd.clone.sunk | while | flops 196611 | bytes 1967404 | solution.py:46
  357.6 54.7 %while.70 = (s32[]{:T(128)}, f32[1,12,64,64]{3,2,1,0:T(8,128)S(1)}, f32[16,1,12,64,64]{4,3,2,1,0:T(8,128)}, f32[16,1,12,1,1]{2,4,3,1,0:T(1,128)S(1)}, f32[16,1,1...) while((s32[]{:T(128)}, f32[1,12,64,64]{3,2,1,0:T(8,128)S(1)}, ...), condition=%wide.region_7.8_spmd.clone, body=%wide.region_6.7_spmd.clone.sunk | while | flops 196611 | bytes 1967404 | solution.py:46
  433.9 29.8 %bitcast_add_fusion.6 = f32[1,16,128,12,64]{2,4,3,1,0:T(8,128)} fusion(f32[16,128,12,64]{1,3,2,0:T(8,128)} %bitcast.635, f32[16,128,12]{1,2,0:T(8,128)S(1)} %copy.646, f32[16,128,12]{1,2,0:T(8,128)S(1)} %copy.636, f32[16,128,128]{2,1,0:T(8,128)} %fusion.217, pred[128,128]{1,0:T(8,128)(4,1)S(1)} %copy-done.110, f32[16,128,12,64]{1,0,3,2:T(8,128)} %bitcast.604), kind=kOutput, calls=%fused_computation.67 | convolution fusion | flops 2431647744 | bytes 20135936 | tf_op jit(solution)/shard_map/jvp(vmap(kijh,kjhp->kihp))/dot_general | solution.py:34
  463.7 29.2 %bitcast_add_fusion.7 = f32[1,16,128,12,64]{2,4,3,1,0:T(8,128)} fusion(f32[16,128,12,64]{1,3,2,0:T(8,128)S(1)} %bitcast.634, f32[16,128,12]{1,2,0:T(8,128)S(1)} %copy-done.53, f32[16,128,12]{1,2,0:T(8,128)S(1)} %copy-done.73, f32[16,128,128]{2,1,0:T(8,128)S(1)} %copy-done.60, pred[128,128]{1,0:T(8,128)(4,1)S(1)} %copy-done.110, ...), kind=kOutput, calls=%fused_computation.68 | convolution fusion | flops 2431647744 | bytes 20135936 | tf_op jit(solution)/shard_map/jvp(vmap(kijh,kjhp->kihp))/dot_general | solution.py:34
  493.6 16.1 copy.672
  551.5 13.7 multiply_reduce_fusion.11
  641.1 51.8 %while.72 = (s32[]{:T(128)}, f32[1,12,64,64]{3,2,1,0:T(8,128)S(1)}, f32[16,1,12]{2,1,0:T(1,128)S(1)}, f32[16,1,12,64,64]{4,3,2,1,0:T(8,128)}, f32[16,1,12,64,64]...) while((s32[]{:T(128)}, f32[1,12,64,64]{3,2,1,0:T(8,128)S(1)}, ...), condition=%wide.region_16.17_spmd.clone, body=%wide.region_14.16_spmd.clone.sunk | while | flops 294904 | bytes 2164048 | solution.py:46
  747.1 51.8 %while.71 = (s32[]{:T(128)}, f32[1,12,64,64]{3,2,1,0:T(8,128)S(1)}, f32[16,1,12]{2,1,0:T(1,128)S(1)}, f32[16,1,12,64,64]{4,3,2,1,0:T(8,128)}, f32[16,1,12,64,64]...) while((s32[]{:T(128)}, f32[1,12,64,64]{3,2,1,0:T(8,128)S(1)}, ...), condition=%wide.region_13.14_spmd.clone, body=%wide.region_11.13_spmd.clone.sunk | while | flops 294904 | bytes 2164048 | solution.py:46
  812.6 15.6 fusion.37
  837.1 27.1 %fusion.62 = f32[16,12,128,128]{3,2,1,0:T(8,128)} fusion(f32[16,12,64,128]{3,0,2,1:T(8,128)} %bitcast.583, f32[16,128,12,64]{1,0,3,2:T(8,128)} %get-tuple-element.853), kind=kOutput, calls=%fused_computation.126 | convolution fusion | flops 2415919104 | bytes 25165824 | tf_op jit(solution)/shard_map/transpose(jvp(vmap(kijh,kjhp->kihp)))/dot_general | solution.py:34
  864.3 20.3 %fusion.36 = (f32[16,128,12]{1,2,0:T(8,128)S(1)}, f32[16,128,12]{1,2,0:T(8,128)}, f32[1,16,128,12,64]{2,4,3,1,0:T(8,128)}) fusion(f32[16,12,64,128]{3,2,1,0:T(8,128)S(1)} %bitcast.655, f32[1,16,128,12,64]{2,1,0,4,3:T(8,128)S(1)} %bitcast.652, f32[16,128,12]{1,2,0:T(8,128)S(1)} %copy-done.82, f32[16,128,12]{1,2,0:T(8,128)S(1)} %copy-done.74, ...), kind=kOutput, calls=%fused_computation.79 | convolution fusion | flops 2439462912 | bytes 26722304 | tf_op jit(solution)/shard_map/transpose(jvp(vmap(kijh,kjhp->kihp)))/dot_general | solution.py:34
  896.7 18.0 %bitcast_add_fusion.5 = f32[1,16,128,12,64]{2,4,3,1,0:T(8,128)S(1)} fusion(f32[16,12,64,128]{3,2,1,0:T(8,128)} %get-tuple-element.906, f32[16,128,12]{1,2,0:T(8,128)S(1)} %copy-done.81, f32[16,128,12]{1,2,0:T(8,128)S(1)} %copy-done.76, f32[16,128,128]{2,1,0:T(8,128)S(1)} %copy-done.62, pred[128,128]{1,0:T(8,128)(4,1)S(1)} %copy-done.110, ...), kind=kOutput, calls=%fused_computation.66 | convolution fusion | flops 2431647744 | bytes 20135936 | tf_op jit(solution)/shard_map/transpose(jvp(vmap(kijh,kjhp->kihp)))/dot_general | solution.py:34
  956.8 41.9 %fusion.19 = (f32[16,128,12]{1,2,0:T(8,128)}, f32[16,128,12]{1,2,0:T(8,128)}, f32[16,128,128]{2,1,0:T(8,128)}, f32[16,128,128]{2,1,0:T(8,128)S(1)}, f32[16,128,12]{1,2,0:T(8,128)}, /*index=5*/f32[16,128,12]{1,2,0:T(8,128)}) fusion(f32[16,128,12]{1,2,0:T(8,128)S(1)} %copy-done.76, f32[16,128,128]{2,1,0:T(8,128)} %fusion.217, ...), kind=kOutput, calls=%fused_computation.53 | convolution fusion | flops 2484502528 | bytes 29966336 | tf_op jit(solution)/shard_map/transpose(jvp(vmap(kijh,kjhp->kihp)))/dot_general | solution.py:34
  1050.2 14.3 multiply_reduce_fusion.4
  1145.4 64.2 %reduce-scatter.12.cloned.1.call-done = f32[1,1024,768]{2,1,0:T(8,128)} async-done(((f32[1,2048,768]{2,1,0:T(8,128)}), f32[1,1024,768]{2,1,0:T(8,128)}) %reduce-scatter.12.cloned.1.call-update) | async-done | bytes 3145744 | tf_op jit(solution)/shard_map/reduce_scatter | solution.py:229
  1215.2 73.9 %reduce-scatter.10.cloned.1.call-done = f32[1,1024,768]{2,1,0:T(8,128)} async-done(((f32[1,2048,768]{2,1,0:T(8,128)}), f32[1,1024,768]{2,1,0:T(8,128)}) %reduce-scatter.10.cloned.1.call-update) | async-done | bytes 3145744 | tf_op jit(solution)/shard_map/reduce_scatter | solution.py:203
  1362.8 102.5 %all-reduce.35.cloned.1.call-done = f32[768,128]{1,0:T(8,128)} async-done(((f32[768,128]{1,0:T(8,128)}), f32[768,128]{1,0:T(8,128)}) %all-reduce.35.cloned.1.call-update) | async-done | bytes 393232 | tf_op jit(solution)/shard_map/psum | solution.py:249
  1471.7 58.2 %all-reduce.28 = (f32[768]{0:T(1024)}, f32[4,768]{1,0:T(4,128)}, f32[4,128]{1,0:T(4,128)}, f32[24]{0:T(128)}, f32[12]{0:T(128)}, /*index=5*/f32[12]{0:T(128)}, f32[768]{0:T(1024)}) all-reduce(f32[768]{0:T(1024)S(1)} %get-tuple-element.843, f32[4,768]{1,0:T(4,128)S(1)} %pad_add_fusion.7, ...), channel_id=1, replica_groups=mesh['dp'=16,'tensor'=2] {'dp'}, use_global_device_ids=true, to_apply=%region_38.39 | all-reduce | flops 5168 | bytes 41344 | tf_op jit(solution)/shard_map/psum | solution.py:249
  1552.9 45.7 %reduce-scatter.16.cloned.1.call-done = f32[48,768]{1,0:T(8,128)} async-done(((f32[768,768]{1,0:T(8,128)}), f32[48,768]{1,0:T(8,128)}) %reduce-scatter.16.cloned.1.call-update) | async-done | bytes 147472 | tf_op jit(solution)/shard_map/reduce_scatter | solution.py:244
  1598.5 66.3 %reduce-scatter.20.cloned.1.call-done = f32[768,48]{0,1:T(8,128)} async-done(((f32[768,768]{0,1:T(8,128)}), f32[768,48]{0,1:T(8,128)}) %reduce-scatter.20.cloned.1.call-update) | async-done | bytes 147472 | tf_op jit(solution)/shard_map/reduce_scatter | solution.py:247
  (916 shorter events, 881.5 us)
Async XLA Ops:
  7.2 133.0 %all-gather.7.cloned.1.call-start = ((), (), s32[]{:S(2)}) async-start(), calls=%async_computation.11 | async-start | bytes 4718592 | tf_op jit(solution)/shard_map/all_gather | solution.py:145
  53.8 80.7 %copy-start.113 = (f32[4,768]{1,0:T(4,128)S(1)}, f32[4,768]{1,0:T(4,128)}, u32[]{:S(2)}) copy-start(f32[4,768]{1,0:T(4,128)} %param.33) | copy-start | bytes 36868
  53.8 81.3 %copy-start.129 = (f32[4,128]{1,0:T(4,128)S(1)}, f32[4,128]{1,0:T(4,128)}, u32[]{:S(2)}) copy-start(f32[4,128]{1,0:T(4,128)} %param.34) | copy-start | bytes 6148
  56.5 83.7 %copy-start.130 = (f32[24]{0:T(128)S(1)}, f32[24]{0:T(128)}, u32[]{:S(2)}) copy-start(f32[24]{0:T(128)} %param.35) | copy-start | bytes 292
  56.5 120.0 %all-gather.9.cloned.1.call-start = ((), (), s32[]{:S(2)}) async-start(), calls=%async_computation.12 | async-start | bytes 1253376 | tf_op jit(solution)/shard_map/all_gather | solution.py:148
  57.3 488.9 %all-gather.11.cloned.1.call-start = ((), (), s32[]{:S(2)}) async-start(), calls=%async_computation.13 | async-start | bytes 1253376 | tf_op jit(solution)/shard_map/all_gather | solution.py:147
  58.0 77.6 %all-to-all-start.2 = ((bf16[16,1,64,768]{3,2,1,0:T(8,128)(2,1)}), bf16[16,1,64,768]{3,2,1,0:T(8,128)(2,1)}, u32[]{:S(2)}, u32[]{:S(2)}) async-start(bf16[16,1,64,768]{3,2,1,0:T(8,128)(2,1)} %param.25), calls=%async_computation.3 | async-start | bytes 3145728 | tf_op jit(solution)/shard_map/all_to_all | solution.py:131
  63.1 502.1 %all-gather.13.cloned.1.call-start = ((), (), s32[]{:S(2)}) async-start(), calls=%async_computation.14 | async-start | bytes 1253376 | tf_op jit(solution)/shard_map/all_gather | solution.py:151
  63.7 501.6 %all-gather.15.cloned.1.call-start = ((), (), s32[]{:S(2)}) async-start(), calls=%async_computation.16 | async-start | bytes 4718592 | tf_op jit(solution)/shard_map/all_gather | solution.py:199
  138.6 966.0 %reduce-scatter.14.cloned.1.call-start = ((), (), s32[]{:S(2)}) async-start(), calls=%async_computation.18 | async-start | bytes 1572864 | tf_op jit(solution)/shard_map/reduce_scatter | solution.py:230
  176.4 138.3 %copy-start.56 = (f32[2048,12]{0,1:T(8,128)}, f32[2048,12]{0,1:T(8,128)S(1)}, u32[]{:S(2)}) copy-start(f32[2048,12]{0,1:T(8,128)S(1)} %get-tuple-element.885) | copy-start | bytes 294916
  1041.3 89.0 %all-reduce.33.cloned.1.call-start = ((), (), s32[]{:S(2)}) async-start(), calls=%async_computation.21 | async-start | bytes 786432 | tf_op jit(solution)/shard_map/psum | solution.py:250
  1107.0 102.7 %reduce-scatter.12.cloned.1.call-start = ((), (), s32[]{:S(2)}) async-start(), calls=%async_computation.17 | async-start | bytes 9437184 | tf_op jit(solution)/shard_map/reduce_scatter | solution.py:229
  1115.5 173.6 %reduce-scatter.10.cloned.1.call-start = ((), (), s32[]{:S(2)}) async-start(), calls=%async_computation.15 | async-start | bytes 9437184 | tf_op jit(solution)/shard_map/reduce_scatter | solution.py:203
  1124.0 237.4 %reduce-scatter.22.cloned.1.call-start = ((), (), s32[]{:S(2)}) async-start(), calls=%async_computation.24 | async-start | bytes 417792
  1127.8 337.5 %all-reduce.35.cloned.1.call-start = ((), (), s32[]{:S(2)}) async-start(), calls=%async_computation.22 | async-start | bytes 786432 | tf_op jit(solution)/shard_map/psum | solution.py:249
  1130.3 422.6 %reduce-scatter.18.cloned.1.call-start = ((), (), s32[]{:S(2)}) async-start(), calls=%async_computation.20 | async-start | bytes 2506752 | tf_op jit(solution)/shard_map/reduce_scatter | solution.py:245
  1137.4 461.2 %reduce-scatter.16.cloned.1.call-start = ((), (), s32[]{:S(2)}) async-start(), calls=%async_computation.19 | async-start | bytes 2506752 | tf_op jit(solution)/shard_map/reduce_scatter | solution.py:244
  1145.4 143.7 %copy-start.97 = (f32[1,1024]{1,0:T(1,128)S(1)}, f32[1,1024]{1,0:T(1,128)}, u32[]{:S(2)}) copy-start(f32[1,1024]{1,0:T(1,128)} %copy-done.96) | copy-start | bytes 12292
  1312.2 39.2 %all-to-all-start.3 = ((bf16[16,2,24576]{2,1,0:T(2,128)(2,1)}), bf16[16,2,24576]{2,1,0:T(2,128)(2,1)S(1)}, u32[]{:S(2)}, u32[]{:S(2)}) async-start(bf16[16,2,24576]{2,1,0:T(2,128)(2,1)} %reshape.1527), calls=%async_computation.6 | async-start | bytes 3145728 | tf_op jit(solution)/shard_map/all_to_all | solution.py:262
  1317.8 347.0 %reduce-scatter.20.cloned.1.call-start = ((), (), s32[]{:S(2)}) async-start(), calls=%async_computation.23 | async-start | bytes 2506752 | tf_op jit(solution)/shard_map/reduce_scatter | solution.py:247
  1329.2 142.4 %copy-start.128 = (f32[12]{0:T(128)S(1)}, f32[12]{0:T(128)}, u32[]{:S(2)}) copy-start(f32[12]{0:T(128)} %get-tuple-element.768) | copy-start | bytes 148
  1351.4 188.1 %all-to-all-start.1 = ((bf16[16,2,24576]{2,1,0:T(2,128)(2,1)}), bf16[16,2,24576]{2,1,0:T(2,128)(2,1)}, u32[]{:S(2)}, u32[]{:S(2)}) async-start(bf16[16,2,24576]{2,1,0:T(2,128)(2,1)} %reshape.1525), calls=%async_computation.2 | async-start | bytes 3145728 | tf_op jit(solution)/shard_map/all_to_all | solution.py:259
  1536.1 128.7 %copy-start.1 = (bf16[16,1,64,768]{3,2,1,0:T(8,128)(2,1)S(1)}, bf16[16,1,64,768]{3,2,1,0:T(8,128)(2,1)}, u32[]{:S(2)}) copy-start(bf16[16,1,64,768]{3,2,1,0:T(8,128)(2,1)} %param.24) | copy-start | bytes 4718596
  (138 other events, 2276.3 us)
Sparse Core Ops, SparseCore 0:
  56.7 45.2 all-gather.6
  104.3 38.4 all-gather.8
  145.1 37.1 all-gather.10
  184.5 37.2 all-gather.12
  223.7 43.8 all-gather.14
  1041.4 17.7 reduce-scatter.13
  1107.1 23.1 all-reduce.32
  1132.6 77.0 reduce-scatter.11
  1212.1 77.0 reduce-scatter.9
  1292.5 67.6 reduce-scatter.21
  1363.9 101.3 all-reduce.34
  1469.5 62.2 reduce-scatter.17
  1536.7 61.8 reduce-scatter.15
  1602.7 62.0 reduce-scatter.19
